TPU v7x, 512 devices: a whole 4x8x8 slice. The times are simulated.
512 devices in a mesh: trow: 32 (over x_hi, z, core), tcol: 16 (over x_lo, y).
Axes of the slice: x: 4 (x_hi: 2, x_lo: 2; x = x_hi * 2 + x_lo), y: 8, z: 8, core: 2. Of those that a mesh axis runs over, the one named last changes fastest.
Arguments:
- start_modes: float32 [1, 32, 16, 512], P(None, 'trow', 'tcol'), may hold values from -0.018 to 0.018
- tiles: float32 [1, 32, 16, 1, 512, 512], P(None, 'trow', 'tcol'), may hold values from -0.046875 to 0.046875
- reach: int32 [1, 32], P(None, 'trow'), may hold values from 2 to 15
- weights: float32 [1, 32, 16, 32], P(None, 'trow', 'tcol'), may hold values from 0.5 to 2
Outputs:
- modes: float32 [1, 32, 16, 512], P(None, 'trow', 'tcol')
Inputs may be any that keep to these rules, and one draw needn't show every extreme that they name: Tile row t uses the stored tiles of offsets 0 to reach of row t; tiles of larger offsets and those left of column 0 are ignored.
All inputs are finite; a program needn't handle non-finite values.
Results may differ from a plain program's by a relative error of at most 0.0001.
Values sent between devices are 32-bit elements; how exact they have to be, the bound alone decides.
A program may use at most 64 MiB of HBM per device.

v0:
```python
import jax
import jax.numpy as jnp
from jax import lax
from jax.sharding import PartitionSpec as P

K = 16
BANDT = 16
ITERS = 2


epsilon = 1e-06


def from_behind(value, axis, steps):
    count = lax.axis_size(axis)
    pairs = [(source, (source + steps) % count) for source in range(count)]
    return lax.ppermute(value, axis, pairs)


def widen(base_slab, shifter):
    row_index = lax.axis_index("trow")
    window = base_slab[None]
    stride = 1
    while stride < BANDT:
        received = shifter(window, stride)
        moved_rows = jnp.concatenate([jnp.zeros_like(received), received[:, :-1]], axis=1)
        received = jnp.where(row_index < stride, moved_rows, received)
        window = jnp.concatenate([window, received], axis=0)
        stride = stride * 2
    return window


def shrink(slot_sums, shifter):
    row_index = lax.axis_index("trow")
    row_devs = lax.axis_size("trow")
    slot_count = slot_sums.shape[0]
    while slot_count > 1:
        half_count = slot_count // 2
        received = shifter(slot_sums[half_count:], -half_count)
        moved_rows = jnp.concatenate([received[:, 1:], jnp.zeros_like(received)], axis=1)
        received = jnp.where(row_index + half_count >= row_devs, moved_rows, received)
        slot_sums = slot_sums[:half_count] + received
        slot_count = half_count
    return slot_sums[0]


def local(start_modes, tiles, reach, weights):
    row_devs = lax.axis_size("trow")
    col_devs = lax.axis_size("tcol")
    row_index = lax.axis_index("trow")
    col_index = lax.axis_index("tcol")
    row_blocks = start_modes.shape[0]
    tile_width = tiles.shape[-1]
    blocks = tiles.shape[3]
    sub_width = tile_width // col_devs
    states = row_blocks * row_devs * tile_width
    local_tiles = tiles.reshape(row_blocks, blocks, tile_width, tile_width)
    lead_offset = (row_index - col_index) % col_devs
    offsets = lead_offset + col_devs * jnp.arange(blocks, dtype=jnp.int32)
    own_ids = jnp.arange(row_blocks, dtype=jnp.int32) * row_devs + row_index
    far_ids = own_ids[:, None] - offsets[None, :]
    present = (offsets[None, :] <= reach) & (far_ids >= 0)
    keep_mask = present.astype(jnp.float32).T[:, :, None, None]
    pop_scale = weights.reshape(row_blocks, sub_width, 1)
    mode_rows = start_modes.reshape(row_blocks, sub_width, K)
    selector = (jnp.arange(col_devs, dtype=jnp.int32) == lead_offset).astype(jnp.float32)
    for sweep in range(ITERS):
        scaled = (mode_rows * pop_scale).reshape(row_blocks, sub_width * K)
        full_slab = lax.all_gather(scaled, "tcol", axis=1, tiled=True)
        window = widen(full_slab, lambda payload, amount: from_behind(payload, "trow", amount))
        grouped = window.reshape(blocks, col_devs, row_blocks, tile_width * K)
        picked = lax.dynamic_index_in_dim(grouped, lead_offset, axis=1, keepdims=False)
        picked = picked.reshape(blocks, row_blocks, tile_width, K)
        own_slab = window[0].reshape(row_blocks, tile_width, K)
        picked = picked * keep_mask
        forward = jnp.einsum("ampq,maqk->apk", local_tiles, picked, precision=lax.Precision.HIGHEST)
        mirror = (
            jnp.einsum("ampq,apk->maqk", local_tiles, own_slab, precision=lax.Precision.HIGHEST)
            * keep_mask
        )
        spread = mirror[:, None] * selector[None, :, None, None, None]
        spread = spread.reshape(BANDT, row_blocks, tile_width, K)
        spread = spread.at[0].add(forward)
        slot_sums = spread.reshape(BANDT, row_blocks, col_devs, sub_width * K)
        folded = shrink(slot_sums, lambda payload, amount: from_behind(payload, "trow", amount))
        summed = lax.psum_scatter(folded, "tcol", scatter_dimension=1, tiled=True)
        values = summed.reshape(row_blocks, sub_width, K) * pop_scale
        flat_rows = values.reshape(row_blocks * sub_width, K)
        local_gram = jnp.dot(
            flat_rows.T,
            flat_rows,
            precision=lax.Precision.HIGHEST,
            preferred_element_type=jnp.float32,
        )
        gram_matrix = lax.psum(local_gram, ("trow", "tcol"))
        gram_matrix = gram_matrix / states + epsilon * jnp.eye(K, dtype=jnp.float32)
        factor = jnp.linalg.cholesky(gram_matrix)
        solved = lax.linalg.triangular_solve(
            factor, flat_rows, left_side=False, lower=True, transpose_a=True
        )
        mode_rows = solved.reshape(row_blocks, sub_width, K)
    return mode_rows.reshape(row_blocks, 1, 1, sub_width * K)


def solution(mesh):
    return jax.shard_map(
        local,
        mesh=mesh,
        in_specs=(
            P(None, "trow", "tcol", None),
            P(None, "trow", "tcol", None, None, None),
            P(None, "trow"),
            P(None, "trow", "tcol", None),
        ),
        out_specs=P(None, "trow", "tcol", None),
        check_vma=False,
    )
```

profile of v0, /device:TPU:1, one launch (start us, length us, event | category | flops | bytes accessed | tf_op | source)
XLA Modules:
  0.0 572.3 jit_solution(16145136578445750278)
XLA Ops:
  1.6 27.6 %all_gather.6 = f32[1,8192]{1,0:T(1,128)S(1)} all-gather(f32[1,512]{1,0:T(1,128)S(1)} %bitcast_multiply_fusion), channel_id=1, replica_groups=mesh['trow'=32,'tcol'=16] {'tcol'}, dimensions={1}, use_global_device_ids=true | all-gather | bytes 34816 | tf_op jit(solution)/shard_map/all_gather | solution.py:69
  29.2 11.8 %collective-permute-start = (f32[1,1,8192]{2,1,0:T(1,128)S(1)}, f32[1,1,8192]{2,1,0:T(1,128)S(1)}, u32[]{:S(2)}, u32[]{:S(2)}) collective-permute-start(f32[1,1,8192]{2,1,0:T(1,128)S(1)} %bitcast.108), channel_id=1, source_target_pairs={{0,16},{16,32},{32,48},{48,64},{64,80},{80,96},{96,112},{112,128},... | collective-permute-start | bytes 98312 | tf_op jit(solution)/shard_map/ppermute | solution.py:17
  42.1 4.0 collective-permute-start.1
  48.1 6.2 %collective-permute-done.1 = f32[2,1,8192]{2,1,0:T(1,128)S(1)} collective-permute-done((f32[2,1,8192]{2,1,0:T(1,128)S(1)}, f32[2,1,8192]{2,1,0:T(1,128)S(1)}, u32[]{:S(2)}, u32[]{:S(2)}) %collective-permute-start.1) | collective-permute-done | bytes 65568 | tf_op jit(solution)/shard_map/ppermute | solution.py:17
  57.1 7.8 %collective-permute-done.2 = f32[4,1,8192]{2,1,0:T(1,128)S(1)} collective-permute-done((f32[4,1,8192]{2,1,0:T(1,128)S(1)}, f32[4,1,8192]{2,1,0:T(1,128)S(1)}, u32[]{:S(2)}, u32[]{:S(2)}) %collective-permute-start.2) | collective-permute-done | bytes 131104 | tf_op jit(solution)/shard_map/ppermute | solution.py:17
  67.4 16.0 %collective-permute-done.3 = f32[8,1,8192]{2,1,0:T(1,128)S(1)} collective-permute-done((f32[8,1,8192]{2,1,0:T(1,128)S(1)}, f32[8,1,8192]{2,1,0:T(1,128)S(1)}, u32[]{:S(2)}, u32[]{:S(2)}) %collective-permute-start.3) | collective-permute-done | bytes 262176 | tf_op jit(solution)/shard_map/ppermute | solution.py:17
  89.4 4.0 collective-permute-start.4
  95.7 10.6 %collective-permute-done.4 = f32[8,1,16,512]{3,2,0,1:T(8,128)} collective-permute-done((f32[8,1,16,512]{3,2,0,1:T(8,128)}, f32[8,1,16,512]{3,2,0,1:T(8,128)}, u32[]{:S(2)}, u32[]{:S(2)}) %collective-permute-start.4) | collective-permute-done | bytes 262176 | tf_op jit(solution)/shard_map/ppermute | solution.py:17
  109.2 5.0 collective-permute-done.5
  116.2 3.1 collective-permute-done.6
  119.3 8.9 %collective-permute-start.7 = (f32[1,1,16,512]{3,2,0,1:T(8,128)S(1)}, f32[1,1,16,512]{3,2,0,1:T(8,128)S(1)}, u32[]{:S(2)}, u32[]{:S(2)}) collective-permute-start(f32[1,1,16,512]{3,2,0,1:T(8,128)S(1)} %slice.150), channel_id=1, source_target_pairs={{0,496},{16,0},{32,16},{48,32},{64,48},{80,64},{96,80},{112,96},{1... | collective-permute-start | bytes 98312 | tf_op jit(solution)/shard_map/ppermute | solution.py:17
  129.6 45.9 %all-reduce = f32[1,16,512]{2,1,0:T(8,128)S(1)} all-reduce(f32[1,16,512]{2,1,0:T(8,128)S(1)} %fusion.14), channel_id=2, replica_groups=mesh['trow'=32,'tcol'=16] {'tcol'}, use_global_device_ids=true, to_apply=%region_0.1.clone | all-reduce | flops 8192 | bytes 65536
  176.6 109.8 %psum.14 = f32[16,16]{0,1:T(8,128)S(1)} all-reduce(f32[16,16]{0,1:T(8,128)S(1)} %fusion.29), channel_id=1, replica_groups=mesh['trow'=32,'tcol'=16] {'trow','tcol'}, use_global_device_ids=true, to_apply=%region_1.2 | all-reduce | flops 256 | bytes 2048 | tf_op jit(solution)/shard_map/psum | solution.py:95
  291.0 23.5 %all_gather.7 = f32[1,8192]{1,0:T(1,128)S(1)} all-gather(f32[1,512]{1,0:T(1,128)S(1)} %reshape.255), channel_id=1, replica_groups=mesh['trow'=32,'tcol'=16] {'tcol'}, dimensions={1}, use_global_device_ids=true | all-gather | bytes 34816 | tf_op jit(solution)/shard_map/all_gather | solution.py:69
  314.5 11.1 %collective-permute-start.8 = (f32[1,1,8192]{2,1,0:T(1,128)S(1)}, f32[1,1,8192]{2,1,0:T(1,128)S(1)}, u32[]{:S(2)}, u32[]{:S(2)}) collective-permute-start(f32[1,1,8192]{2,1,0:T(1,128)S(1)} %bitcast.112), channel_id=1, source_target_pairs={{0,16},{16,32},{32,48},{48,64},{64,80},{80,96},{96,112},{112,128},... | collective-permute-start | bytes 98312 | tf_op jit(solution)/shard_map/ppermute | solution.py:17
  328.7 6.7 %collective-permute-done.9 = f32[2,1,8192]{2,1,0:T(1,128)S(1)} collective-permute-done((f32[2,1,8192]{2,1,0:T(1,128)S(1)}, f32[2,1,8192]{2,1,0:T(1,128)S(1)}, u32[]{:S(2)}, u32[]{:S(2)}) %collective-permute-start.9) | collective-permute-done | bytes 65568 | tf_op jit(solution)/shard_map/ppermute | solution.py:17
  338.4 7.6 %collective-permute-done.10 = f32[4,1,8192]{2,1,0:T(1,128)S(1)} collective-permute-done((f32[4,1,8192]{2,1,0:T(1,128)S(1)}, f32[4,1,8192]{2,1,0:T(1,128)S(1)}, u32[]{:S(2)}, u32[]{:S(2)}) %collective-permute-start.10) | collective-permute-done | bytes 131104 | tf_op jit(solution)/shard_map/ppermute | solution.py:17
  349.2 14.0 %collective-permute-done.11 = f32[8,1,8192]{2,1,0:T(1,128)S(1)} collective-permute-done((f32[8,1,8192]{2,1,0:T(1,128)S(1)}, f32[8,1,8192]{2,1,0:T(1,128)S(1)}, u32[]{:S(2)}, u32[]{:S(2)}) %collective-permute-start.11) | collective-permute-done | bytes 262176 | tf_op jit(solution)/shard_map/ppermute | solution.py:17
  373.3 7.3 %collective-permute-done.12 = f32[8,1,16,512]{3,2,0,1:T(8,128)} collective-permute-done((f32[8,1,16,512]{3,2,0,1:T(8,128)}, f32[8,1,16,512]{3,2,0,1:T(8,128)}, u32[]{:S(2)}, u32[]{:S(2)}) %collective-permute-start.12) | collective-permute-done | bytes 262176 | tf_op jit(solution)/shard_map/ppermute | solution.py:17
  383.6 5.1 collective-permute-done.13
  390.6 3.1 collective-permute-done.14
  393.7 12.5 %collective-permute-start.15 = (f32[1,1,16,512]{3,2,0,1:T(8,128)S(1)}, f32[1,1,16,512]{3,2,0,1:T(8,128)S(1)}, u32[]{:S(2)}, u32[]{:S(2)}) collective-permute-start(f32[1,1,16,512]{3,2,0,1:T(8,128)S(1)} %slice.159), channel_id=1, source_target_pairs={{0,496},{16,0},{32,16},{48,32},{64,48},{80,64},{96,80},{112,96},{1... | collective-permute-start | bytes 98312 | tf_op jit(solution)/shard_map/ppermute | solution.py:17
  407.1 49.7 %all-reduce.1 = f32[1,16,512]{2,1,0:T(8,128)S(1)} all-reduce(f32[1,16,512]{2,1,0:T(8,128)S(1)} %fusion.13), channel_id=3, replica_groups=mesh['trow'=32,'tcol'=16] {'tcol'}, use_global_device_ids=true, to_apply=%region_4.7.clone | all-reduce | flops 8192 | bytes 65536
  458.0 109.2 %psum.15 = f32[16,16]{0,1:T(8,128)S(1)} all-reduce(f32[16,16]{0,1:T(8,128)S(1)} %fusion.30), channel_id=1, replica_groups=mesh['trow'=32,'tcol'=16] {'trow','tcol'}, use_global_device_ids=true, to_apply=%region_5.8 | all-reduce | flops 256 | bytes 2048 | tf_op jit(solution)/shard_map/psum | solution.py:95
  (111 shorter events, 60.4 us)
Async XLA Ops:
  0.0 56.5 %copy-start = (f32[1,1,1,1,512,512]{5,4,3,2,1,0:T(8,128)S(1)}, f32[1,1,1,1,512,512]{5,4,3,2,1,0:T(8,128)}, u32[]{:S(2)}) copy-start(f32[1,1,1,1,512,512]{5,4,3,2,1,0:T(8,128)} %param.12) | copy-start | bytes 3145732
  29.2 12.8 %collective-permute-start = (f32[1,1,8192]{2,1,0:T(1,128)S(1)}, f32[1,1,8192]{2,1,0:T(1,128)S(1)}, u32[]{:S(2)}, u32[]{:S(2)}) collective-permute-start(f32[1,1,8192]{2,1,0:T(1,128)S(1)} %bitcast.108), channel_id=1, source_target_pairs={{0,16},{16,32},{32,48},{48,64},{64,80},{80,96},{96,112},{112,128},... | collective-permute-start | bytes 98312 | tf_op jit(solution)/shard_map/ppermute | solution.py:17
  42.1 12.2 %collective-permute-start.1 = (f32[2,1,8192]{2,1,0:T(1,128)S(1)}, f32[2,1,8192]{2,1,0:T(1,128)S(1)}, u32[]{:S(2)}, u32[]{:S(2)}) collective-permute-start(f32[2,1,8192]{2,1,0:T(1,128)S(1)} %pad_maximum_fusion.4), channel_id=1, source_target_pairs={{0,32},{16,48},{32,64},{48,80},{64,96},{80,112},{96,128},{112,144}... | collective-permute-start | bytes 196616 | tf_op jit(solution)/shard_map/ppermute | solution.py:17
  54.5 10.4 %collective-permute-start.2 = (f32[4,1,8192]{2,1,0:T(1,128)S(1)}, f32[4,1,8192]{2,1,0:T(1,128)S(1)}, u32[]{:S(2)}, u32[]{:S(2)}) collective-permute-start(f32[4,1,8192]{2,1,0:T(1,128)S(1)} %pad_maximum_fusion.2), channel_id=1, source_target_pairs={{0,64},{16,80},{32,96},{48,112},{64,128},{80,144},{96,160},{112,17... | collective-permute-start | bytes 393224 | tf_op jit(solution)/shard_map/ppermute | solution.py:17
  65.4 18.0 %collective-permute-start.3 = (f32[8,1,8192]{2,1,0:T(1,128)S(1)}, f32[8,1,8192]{2,1,0:T(1,128)S(1)}, u32[]{:S(2)}, u32[]{:S(2)}) collective-permute-start(f32[8,1,8192]{2,1,0:T(1,128)S(1)} %pad_maximum_fusion), channel_id=1, source_target_pairs={{0,128},{16,144},{32,160},{48,176},{64,192},{80,208},{96,224},{112... | collective-permute-start | bytes 786440 | tf_op jit(solution)/shard_map/ppermute | solution.py:17
  89.4 16.8 %collective-permute-start.4 = (f32[8,1,16,512]{3,2,0,1:T(8,128)}, f32[8,1,16,512]{3,2,0,1:T(8,128)}, u32[]{:S(2)}, u32[]{:S(2)}) collective-permute-start(f32[8,1,16,512]{3,2,0,1:T(8,128)} %slice.124), channel_id=1, source_target_pairs={{0,384},{16,400},{32,416},{48,432},{64,448},{80,464},{96,480},{112... | collective-permute-start | bytes 786440 | tf_op jit(solution)/shard_map/ppermute | solution.py:17
  94.1 196.6 %copy-start.1 = (f32[1,1,1,32]{3,2,1,0:T(1,128)S(1)}, f32[1,1,1,32]{3,2,1,0:T(1,128)}, u32[]{:S(2)}) copy-start(f32[1,1,1,32]{3,2,1,0:T(1,128)} %param.14) | copy-start | bytes 388
  107.2 7.0 %collective-permute-start.5 = (f32[4,1,16,512]{3,2,0,1:T(8,128)S(1)}, f32[4,1,16,512]{3,2,0,1:T(8,128)S(1)}, u32[]{:S(2)}, u32[]{:S(2)}) collective-permute-start(f32[4,1,16,512]{3,2,0,1:T(8,128)S(1)} %slice.146), channel_id=1, source_target_pairs={{0,448},{16,464},{32,480},{48,496},{64,0},{80,16},{96,32},{112,48}... | collective-permute-start | bytes 393224 | tf_op jit(solution)/shard_map/ppermute | solution.py:17
  114.2 5.0 collective-permute-start.6
  119.3 10.3 %collective-permute-start.7 = (f32[1,1,16,512]{3,2,0,1:T(8,128)S(1)}, f32[1,1,16,512]{3,2,0,1:T(8,128)S(1)}, u32[]{:S(2)}, u32[]{:S(2)}) collective-permute-start(f32[1,1,16,512]{3,2,0,1:T(8,128)S(1)} %slice.150), channel_id=1, source_target_pairs={{0,496},{16,0},{32,16},{48,32},{64,48},{80,64},{96,80},{112,96},{1... | collective-permute-start | bytes 98312 | tf_op jit(solution)/shard_map/ppermute | solution.py:17
  314.5 12.2 %collective-permute-start.8 = (f32[1,1,8192]{2,1,0:T(1,128)S(1)}, f32[1,1,8192]{2,1,0:T(1,128)S(1)}, u32[]{:S(2)}, u32[]{:S(2)}) collective-permute-start(f32[1,1,8192]{2,1,0:T(1,128)S(1)} %bitcast.112), channel_id=1, source_target_pairs={{0,16},{16,32},{32,48},{48,64},{64,80},{80,96},{96,112},{112,128},... | collective-permute-start | bytes 98312 | tf_op jit(solution)/shard_map/ppermute | solution.py:17
  326.8 8.6 %collective-permute-start.9 = (f32[2,1,8192]{2,1,0:T(1,128)S(1)}, f32[2,1,8192]{2,1,0:T(1,128)S(1)}, u32[]{:S(2)}, u32[]{:S(2)}) collective-permute-start(f32[2,1,8192]{2,1,0:T(1,128)S(1)} %pad_maximum_fusion.5), channel_id=1, source_target_pairs={{0,32},{16,48},{32,64},{48,80},{64,96},{80,112},{96,128},{112,144}... | collective-permute-start | bytes 196616 | tf_op jit(solution)/shard_map/ppermute | solution.py:17
  335.6 10.3 %collective-permute-start.10 = (f32[4,1,8192]{2,1,0:T(1,128)S(1)}, f32[4,1,8192]{2,1,0:T(1,128)S(1)}, u32[]{:S(2)}, u32[]{:S(2)}) collective-permute-start(f32[4,1,8192]{2,1,0:T(1,128)S(1)} %pad_maximum_fusion.3), channel_id=1, source_target_pairs={{0,64},{16,80},{32,96},{48,112},{64,128},{80,144},{96,160},{112,17... | collective-permute-start | bytes 393224 | tf_op jit(solution)/shard_map/ppermute | solution.py:17
  346.4 16.9 %collective-permute-start.11 = (f32[8,1,8192]{2,1,0:T(1,128)S(1)}, f32[8,1,8192]{2,1,0:T(1,128)S(1)}, u32[]{:S(2)}, u32[]{:S(2)}) collective-permute-start(f32[8,1,8192]{2,1,0:T(1,128)S(1)} %pad_maximum_fusion.1), channel_id=1, source_target_pairs={{0,128},{16,144},{32,160},{48,176},{64,192},{80,208},{96,224},{112... | collective-permute-start | bytes 786440 | tf_op jit(solution)/shard_map/ppermute | solution.py:17
  369.3 11.4 %collective-permute-start.12 = (f32[8,1,16,512]{3,2,0,1:T(8,128)}, f32[8,1,16,512]{3,2,0,1:T(8,128)}, u32[]{:S(2)}, u32[]{:S(2)}) collective-permute-start(f32[8,1,16,512]{3,2,0,1:T(8,128)} %slice.135), channel_id=1, source_target_pairs={{0,384},{16,400},{32,416},{48,432},{64,448},{80,464},{96,480},{112... | collective-permute-start | bytes 786440 | tf_op jit(solution)/shard_map/ppermute | solution.py:17
  381.7 7.0 %collective-permute-start.13 = (f32[4,1,16,512]{3,2,0,1:T(8,128)S(1)}, f32[4,1,16,512]{3,2,0,1:T(8,128)S(1)}, u32[]{:S(2)}, u32[]{:S(2)}) collective-permute-start(f32[4,1,16,512]{3,2,0,1:T(8,128)S(1)} %slice.155), channel_id=1, source_target_pairs={{0,448},{16,464},{32,480},{48,496},{64,0},{80,16},{96,32},{112,48}... | collective-permute-start | bytes 393224 | tf_op jit(solution)/shard_map/ppermute | solution.py:17
  388.7 5.0 collective-permute-start.14
  393.7 13.4 %collective-permute-start.15 = (f32[1,1,16,512]{3,2,0,1:T(8,128)S(1)}, f32[1,1,16,512]{3,2,0,1:T(8,128)S(1)}, u32[]{:S(2)}, u32[]{:S(2)}) collective-permute-start(f32[1,1,16,512]{3,2,0,1:T(8,128)S(1)} %slice.159), channel_id=1, source_target_pairs={{0,496},{16,0},{32,16},{48,32},{64,48},{80,64},{96,80},{112,96},{1... | collective-permute-start | bytes 98312 | tf_op jit(solution)/shard_map/ppermute | solution.py:17
where the time goes:
time: 573 us; the launch traced here: 572 us
  blocking collectives  366 us (64%)
  waiting for transfers between devices  95.2 us (17%)
  starting transfers between devices  71.8 us (13%)
  local copies, waits for them, and re-layouts  18.2 us (3%)
  other arithmetic  15.9 us (3%)
    psum x2, blocking collectives, local(): gram_matrix = lax.psum(local_gram, ('trow', 'tcol'))  219 us
    unnamed x2, blocking collectives  95.7 us
    ppermute x16, waiting for transfers between devices, from_behind(): return lax.ppermute(value, axis, pairs)  95.2 us
    ppermute x16, starting transfers between devices, from_behind(): return lax.ppermute(value, axis, pairs)  71.8 us
    all_gather x2, blocking collectives, local(): full_slab = lax.all_gather(scaled, 'tcol', axis=1, tiled=True)  51.1 us
  transfers between devices with their start and end apart: 16, of which 15 were waited for; matrix products, arithmetic and copies ran while one was open for 2% of the time, Pallas kernels for 0%

commit v1 on v0

v1 whole, which is shorter than its diff:
```python
import functools

import jax
import jax.numpy as jnp
from jax import lax
from jax.experimental import pallas as pl
from jax.experimental.pallas import tpu as pltpu
from jax.sharding import PartitionSpec as P

K = 16
SUB = 32
EPS = 1e-06
F32 = jnp.float32
BF16 = jnp.bfloat16
MESH = pl.DeviceIdType.MESH
NT = (((1,), (1,)), ((), ()))
NN = (((1,), (0,)), ((), ()))


def iota(shape, axis):
    return lax.broadcasted_iota(jnp.int32, shape, axis)


def dot_half(a, b, dims):
    return lax.dot_general(a, b, dims, preferred_element_type=F32)


def swap_blocks(block):
    top, bottom = block[0:8], block[8:16]
    lane = iota((8, 128), 1)
    row = iota((8, 128), 0)
    low = lane < 64
    halves = (
        jnp.where(low, top, pltpu.roll(bottom, 64, 1)),
        jnp.where(low, pltpu.roll(top, 64, 1), bottom),
    )
    odd_lane = (lane // 32) % 2
    odd_row = row // 4
    done = []
    for half in halves:
        turned = pltpu.roll(half, 4, 0)
        moved = jnp.where(odd_lane == 1, pltpu.roll(turned, 32, 1), pltpu.roll(turned, 96, 1))
        done.append(jnp.where(odd_lane == odd_row, half, moved))
    return jnp.concatenate(done, axis=0)


def slab_to_vectors(slab):
    flat = slab.reshape(slab.shape[0] * 4, 128)
    return jnp.concatenate(
        [swap_blocks(flat[16 * i : 16 * i + 16]) for i in range(slab.shape[0] // 4)], axis=1
    )


def fold_lanes(value, shifts):
    for shift in shifts:
        value = value + pltpu.roll(value, shift, 1)
    return value


def rows_spread(packed):
    count = packed.shape[0]
    wide = jnp.concatenate(
        [jnp.broadcast_to(packed[a : a + 1], (8, 128)) for a in range(count)], axis=0
    )
    shape = (8 * count, 128)
    keep = iota(shape, 1) // 16 == iota(shape, 0) % 8
    return fold_lanes(jnp.where(keep, wide, 0.0), (64, 32, 16))


def rows_packed(spread):
    shape = spread.shape
    keep = iota(shape, 1) // 16 == iota(shape, 0) % 8
    held = jnp.where(keep, spread, 0.0)
    return jnp.concatenate(
        [jnp.sum(held[8 * a : 8 * a + 8], axis=0, keepdims=True) for a in range(shape[0] // 8)],
        axis=0,
    )


def split(value):
    high = value.astype(BF16)
    return high, (value - high.astype(F32)).astype(BF16)


def dot_split(a_parts, b_parts, dims):
    rows = a_parts[0].shape[0]
    both = dot_half(jnp.concatenate(a_parts, axis=0), b_parts[0], dims)
    return both[0:rows] + (both[rows:] + dot_half(a_parts[0], b_parts[1], dims))


def gram_spread(vectors):
    parts = split(vectors)
    return dot_split(parts, [jnp.concatenate([part] * 8, axis=0) for part in parts], NT)


def inverse_factor(gram):
    row = iota((8, 128), 0)
    tops = [jnp.broadcast_to(gram[0:8, k : k + 1], (8, 128)) for k in range(K)]
    bottoms = [jnp.broadcast_to(gram[8:16, k : k + 1], (8, 128)) for k in range(K)]
    unit = iota((8, 128), 1) % K
    right = [jnp.where(unit == row, 1.0, 0.0), jnp.where(unit == row + 8, 1.0, 0.0)]
    scale = [jnp.zeros((8, 128), F32), jnp.zeros((8, 128), F32)]
    for step in range(K):
        half, place = step // 8, step % 8
        here = (tops, bottoms)[half]
        pivot = here[step][place : place + 1]
        scale[half] = jnp.where(row == place, lax.rsqrt(pivot), scale[half])
        if step == K - 1:
            break
        inverse = 1.0 / pivot
        lines = [here[k][place : place + 1] for k in range(K)]
        right_line = right[half][place : place + 1]
        if step < 7:
            factor = jnp.where(row > place, tops[step] * inverse, 0.0)
            for k in range(step + 1, K):
                tops[k] = tops[k] - factor * lines[k]
            right[0] = right[0] - factor * right_line
        factor = bottoms[step] * inverse
        if half == 1:
            factor = jnp.where(row > place, factor, 0.0)
        for k in range(step + 1, K):
            bottoms[k] = bottoms[k] - factor * lines[k]
        right[1] = right[1] - factor * right_line
    return jnp.concatenate([right[0] * scale[0], right[1] * scale[1]], axis=0)


def far_first(count, period):
    return sorted(range(1, count), key=lambda o: (-min(o % period, period - o % period), o))


def kernel(
    n_row,
    n_col,
    states,
    x_hbm,
    tile_hbm,
    reach_hbm,
    weight_hbm,
    out_ref,
    x_ref,
    tile_ref,
    reach_ref,
    weight_ref,
    high_ref,
    low_ref,
    weight_row_ref,
    weight_parts_ref,
    chunk_weight_ref,
    z_ref,
    slab_ref,
    own_ref,
    far_ref,
    parts_ref,
    chunk_ref,
    wide_ref,
    gram_first_ref,
    gram_ref,
    gram_row_ref,
    gram_col_ref,
    result_ref,
    back_ref,
    load_sem,
    weight_sem,
    z_row_sem,
    z_col_sem,
    part_sem,
    gram_sem,
    back_sem,
    weight_sent,
    z_sent,
    own_sent,
    far_sent,
    gram_sent,
    back_sent,
):
    r = lax.axis_index("trow")
    c = lax.axis_index("tcol")
    chunks = n_col // 4
    home = lax.rem(r, n_col)
    d = lax.rem(r - c + n_row, n_col)
    j = lax.rem(r - d + n_row, n_row)
    off_diagonal = d != 0
    y_count = n_col // 2

    def owner(row, chunk):
        place = lax.rem(row, n_col)
        x_low = lax.rem(lax.div(place, y_count) + lax.div(chunk, 2), 2)
        return x_low * y_count + lax.rem(place + y_count - 1 + 2 * lax.rem(chunk, 2), y_count)

    owners = [owner(r, i) for i in range(chunks)]
    mine = sum(jnp.where(c == place, i, 0) for i, place in enumerate(owners))
    is_owner = functools.reduce(jnp.logical_or, [c == place for place in owners])
    not_owner = jnp.logical_not(is_owner)

    def push(source, target, sent, arrived, device):
        pltpu.make_async_remote_copy(
            src_ref=source,
            dst_ref=target,
            send_sem=sent,
            recv_sem=arrived,
            device_id=device,
            device_id_type=MESH,
        ).start()

    def wait_for(ref, sem):
        pltpu.make_async_copy(ref, ref, sem).wait()

    def user(o):
        return lax.rem(r + o, n_row), home

    def peer(o):
        return r, lax.rem(c + o, n_col)

    peers = far_first(n_col, y_count)
    users = far_first(n_col, n_col)

    loads = [
        pltpu.make_async_copy(source, target, load_sem.at[i])
        for i, (source, target) in enumerate(
            ((x_hbm, x_ref), (weight_hbm, weight_ref), (reach_hbm, reach_ref), (tile_hbm, tile_ref))
        )
    ]
    for load in loads:
        load.start()

    barrier = pltpu.get_barrier_semaphore()

    def greet(device):
        pl.semaphore_signal(barrier, inc=1, device_id=device, device_id_type=MESH)

    @pl.when(off_diagonal)
    def _():
        for o in range(n_col):
            greet((j, o))

    @pl.when(is_owner)
    def _():
        for o in users:
            greet(user(o))

    for o in peers:
        greet(peer(o))

    loads[0].wait()
    loads[1].wait()
    spread = rows_spread(x_ref[...])
    turned = jnp.transpose(jnp.concatenate([spread] * 4, axis=0))[0:16]
    weight = jnp.concatenate([weight_ref[...]] * 4, axis=1)
    scaled = jnp.where(iota((16, 128), 1) // 32 == iota((16, 128), 0) // 4, turned * weight, 0.0)
    eight = scaled[0:8] + scaled[8:16]
    piece = eight[0:4] + eight[4:8]
    z_ref[...] = piece
    slab_ref[0, c] = piece
    weight_row_ref[...] = weight

    pl.semaphore_wait(barrier, 2 * (n_col - 1) + jnp.where(off_diagonal, chunks, 0))
    for o in peers:
        push(z_ref, slab_ref.at[0, c], z_sent.at[0], z_row_sem.at[0], peer(o))
    for o in users:
        push(z_ref, slab_ref.at[1, c], z_sent.at[0], z_col_sem.at[0], user(o))

    group, slot = lax.div(c, 4), lax.rem(c, 4)
    keeper = owner(r, group)

    @pl.when(c == keeper)
    def _():
        weight_parts_ref[slot] = weight

    @pl.when(c != keeper)
    def _():
        push(weight_row_ref, weight_parts_ref.at[slot], weight_sent, weight_sem, (r, keeper))

    loads[2].wait()
    loads[3].wait()
    keep = jnp.where(d <= reach_ref[...], 1.0, 0.0) * jnp.where(r >= d, 1.0, 0.0)
    tile = tile_ref[...] * keep
    high_ref[0], low_ref[0] = split(tile)
    high_ref[1], low_ref[1] = split(jnp.transpose(tile))
    lone = jnp.where(off_diagonal, 0.0, 1.0)

    def multiply(sweep, near, far_vectors):
        mirror = dot_split(split(near), (high_ref[0], low_ref[0]), NN)
        for i in range(chunks):
            far_ref[sweep, i] = mirror[:, 128 * i : 128 * i + 128]

        @pl.when(off_diagonal)
        def _():
            for turn in range(chunks):
                i = lax.rem(d + turn, chunks)
                push(
                    far_ref.at[sweep, i],
                    parts_ref.at[sweep, n_col - 2 + d],
                    far_sent.at[sweep],
                    part_sem.at[sweep],
                    (j, owner(j, i)),
                )

        forward = dot_split(split(far_vectors()), (high_ref[1], low_ref[1]), NN) + lone * mirror
        for i in range(chunks):
            own_ref[sweep, i] = forward[:, 128 * i : 128 * i + 128]
        for turn in range(chunks):
            i = lax.rem(c + turn, chunks)
            place = owner(r, i)

            @pl.when(c != place)
            def _():
                push(
                    own_ref.at[sweep, i],
                    parts_ref.at[sweep, lax.rem(place - c + n_col, n_col) - 1],
                    own_sent.at[sweep],
                    part_sem.at[sweep],
                    (r, place),
                )

    def total(sweep):
        wait_for(parts_ref.at[sweep], part_sem.at[sweep])
        return own_ref[sweep, mine] + jnp.sum(parts_ref[sweep], axis=0)

    side = jnp.where(off_diagonal, 1, 0)

    wait_for(slab_ref.at[0, pl.ds(0, n_col - 1)], z_row_sem.at[0])

    def far_pieces():
        @pl.when(off_diagonal)
        def _():
            wait_for(slab_ref.at[1], z_col_sem.at[0])

        return slab_to_vectors(slab_ref[side])

    multiply(0, slab_to_vectors(slab_ref[0]), far_pieces)

    @pl.when(is_owner)
    def _():
        inside = mine == group

        @pl.when(inside)
        def _():
            wait_for(weight_parts_ref.at[pl.ds(0, 3)], weight_sem)

        @pl.when(jnp.logical_not(inside))
        def _():
            wait_for(weight_parts_ref, weight_sem)

        lane = iota((1, 128), 1) // SUB
        chunk_weight = sum(jnp.where(lane == i, weight_parts_ref[i], 0.0) for i in range(4))
        chunk_weight_ref[...] = chunk_weight
        values = total(0) * chunk_weight
        scaled = values * chunk_weight
        chunk_ref[...] = scaled
        wide_ref[0, mine] = scaled
        for o in peers:
            push(chunk_ref, wide_ref.at[0, mine], z_sent.at[1], z_row_sem.at[1], peer(o))
        for o in users:
            push(chunk_ref, wide_ref.at[1, mine], z_sent.at[1], z_col_sem.at[1], user(o))
        gram_first_ref[...] = gram_spread(values)
        if chunks > 1:
            wait_for(wide_ref.at[0, pl.ds(0, chunks - 1)], z_row_sem.at[1])

    @pl.when(not_owner)
    def _():
        wait_for(wide_ref.at[0], z_row_sem.at[1])

    def far_chunks():
        @pl.when(off_diagonal)
        def _():
            wait_for(wide_ref.at[1], z_col_sem.at[1])

        return jnp.concatenate([wide_ref[side, i] for i in range(chunks)], axis=1)

    multiply(1, jnp.concatenate([wide_ref[0, i] for i in range(chunks)], axis=1), far_chunks)

    @pl.when(is_owner)
    def _():
        values = total(1) * chunk_weight_ref[...]
        gram = rows_packed(gram_spread(values) + EPS * gram_first_ref[...])
        gram_ref[0] = gram
        gram_row_ref[mine] = gram
        for o in peers:
            push(gram_ref.at[0], gram_row_ref.at[mine], gram_sent.at[0], gram_sem.at[0], peer(o))
        turned = jnp.transpose(jnp.concatenate([values] * 8, axis=0))
        result_ref[...] = rows_packed(turned).reshape(4, 4, 128)
        for i in range(4):
            place = 4 * mine + i

            @pl.when(c == place)
            def _():
                back_ref[...] = result_ref[i]

            @pl.when(c != place)
            def _():
                push(result_ref.at[i], back_ref, back_sent, back_sem, (r, place))

        if chunks > 1:
            wait_for(gram_row_ref.at[pl.ds(0, chunks - 1)], gram_sem.at[0])

    @pl.when(not_owner)
    def _():
        wait_for(gram_row_ref, gram_sem.at[0])

    gram_own = jnp.sum(gram_row_ref[...], axis=0)
    gram_ref[1] = gram_own
    for o in far_first(n_row, n_col):
        row = lax.rem(r + o, n_row)
        push(gram_ref.at[1], gram_col_ref.at[o - 1], gram_sent.at[1], gram_sem.at[1], (row, c))

    @pl.when(c != keeper)
    def _():
        wait_for(back_ref, back_sem)

    back = split(jnp.concatenate([back_ref[...]] * 4, axis=0))
    wait_for(gram_col_ref, gram_sem.at[1])
    gram = rows_spread(gram_own + jnp.sum(gram_col_ref[...], axis=0))
    diagonal = jnp.where(iota((16, 128), 1) % K == iota((16, 128), 0), EPS * EPS, 0.0)
    solver = inverse_factor(gram * (1.0 / states) + diagonal)
    wide = jnp.concatenate([solver] * 8, axis=0)
    wide = jnp.where(iota((128, 128), 0) // K == iota((128, 128), 1) // K, wide, 0.0)
    out_ref[...] = dot_split(back, split(wide), NT)[0:4]

    wait_for(slab_ref.at[:, pl.ds(0, n_col - 1)], z_sent.at[0])
    wait_for(gram_col_ref, gram_sent.at[1])

    @pl.when(c != keeper)
    def _():
        wait_for(weight_row_ref, weight_sent)

    for sweep in range(2):

        @pl.when(off_diagonal)
        def _():
            wait_for(far_ref.at[sweep], far_sent.at[sweep])

        @pl.when(is_owner)
        def _():
            if chunks > 1:
                wait_for(own_ref.at[sweep, pl.ds(0, chunks - 1)], own_sent.at[sweep])

        @pl.when(not_owner)
        def _():
            wait_for(own_ref.at[sweep], own_sent.at[sweep])

    @pl.when(is_owner)
    def _():
        wait_for(parts_ref.at[0], z_sent.at[1])
        wait_for(gram_col_ref.at[pl.ds(0, n_col - 1)], gram_sent.at[0])

        @pl.when(mine == group)
        def _():
            wait_for(result_ref.at[pl.ds(0, 3)], back_sent)

        @pl.when(mine != group)
        def _():
            wait_for(result_ref, back_sent)


def local(start_modes, tiles, reach, weights, n_row, n_col):
    width = tiles.shape[-1]
    chunks = n_col // 4
    dma = pltpu.SemaphoreType.DMA
    out = pl.pallas_call(
        functools.partial(kernel, n_row, n_col, n_row * width),
        out_shape=pltpu.VMEM((4, 128), F32),
        in_specs=[pl.BlockSpec(memory_space=pltpu.HBM)] * 4,
        out_specs=pl.BlockSpec(memory_space=pltpu.VMEM),
        scratch_shapes=[
            pltpu.VMEM((4, 128), F32),
            pltpu.VMEM((width, width), F32),
            pltpu.VMEM((1, 1), jnp.int32),
            pltpu.VMEM((1, SUB), F32),
            pltpu.VMEM((2, width, width), BF16),
            pltpu.VMEM((2, width, width), BF16),
            pltpu.VMEM((1, 128), F32),
            pltpu.VMEM((4, 1, 128), F32),
            pltpu.VMEM((1, 128), F32),
            pltpu.VMEM((4, 128), F32),
            pltpu.VMEM((2, n_col, 4, 128), F32),
            pltpu.VMEM((2, chunks, K, 128), F32),
            pltpu.VMEM((2, chunks, K, 128), F32),
            pltpu.VMEM((2, 2 * (n_col - 1), K, 128), F32),
            pltpu.VMEM((K, 128), F32),
            pltpu.VMEM((2, chunks, K, 128), F32),
            pltpu.VMEM((K, 128), F32),
            pltpu.VMEM((2, 2, 128), F32),
            pltpu.VMEM((chunks, 2, 128), F32),
            pltpu.VMEM((n_row - 1, 2, 128), F32),
            pltpu.VMEM((4, 4, 128), F32),
            pltpu.VMEM((4, 128), F32),
            dma((4,)),
            dma(()),
            dma((2,)),
            dma((2,)),
            dma((2,)),
            dma((2,)),
            dma(()),
            dma(()),
            dma((2,)),
            dma((2,)),
            dma((2,)),
            dma((2,)),
            dma(()),
        ],
        compiler_params=pltpu.CompilerParams(
            collective_id=0, has_side_effects=True, vmem_limit_bytes=60 * 1024 * 1024
        ),
    )(
        start_modes.reshape(4, 128),
        tiles.reshape(width, width),
        reach,
        weights.reshape(1, SUB),
    )
    return out.reshape(start_modes.shape)


def solution(mesh):
    return jax.shard_map(
        functools.partial(local, n_row=mesh.shape["trow"], n_col=mesh.shape["tcol"]),
        mesh=mesh,
        in_specs=(
            P(None, "trow", "tcol", None),
            P(None, "trow", "tcol", None, None, None),
            P(None, "trow"),
            P(None, "trow", "tcol", None),
        ),
        out_specs=P(None, "trow", "tcol", None),
        check_vma=False,
    )
```

time: 573 us -> 53.9 us (0.09)
  blocking collectives: 366 us -> 0 us
  waiting for transfers between devices: 95.2 us -> 0 us
  starting transfers between devices: 71.8 us -> 0 us
  Pallas kernels: 0 us -> 52.5 us
  local copies, waits for them, and re-layouts: 18.2 us -> 0.58 us
  other arithmetic: 15.9 us -> 0 us
    psum x2 -> x0, blocking collectives: 219 us -> none  [local(): gram_matrix = lax.psum(local_gram, ('trow', 'tcol'))]
    unnamed x2 -> x0, blocking collectives: 95.7 us -> none
    ppermute x16 -> x0, waiting for transfers between devices: 95.2 us -> none  [from_behind(): return lax.ppermute(value, axis, pairs)]
    ppermute x16 -> x0, starting transfers between devices: 71.8 us -> none  [from_behind(): return lax.ppermute(value, axis, pairs)]
    pallas_call x0 -> x1, Pallas kernels: none -> 52.5 us  [local(): pl.pallas_call(functools.partial(kernel, n_row, n_col, n_row * width), ou...]
    all_gather x2 -> x0, blocking collectives: 51.1 us -> none  [local(): full_slab = lax.all_gather(scaled, 'tcol', axis=1, tiled=True)]
    slice x16 -> x0, local copies, waits for them, and re-layouts: 13.4 us -> none  [the longest x12 9.14 us: shrink(): received = shifter(slot_sums[half_count:], -half_count)]
    another operation x10 -> x0, other arithmetic: 8.13 us -> none  [the longest x6 4.34 us: local(): factor = jnp.linalg.cholesky(gram_matrix)]
  transfers between devices with their start and end apart: 16 -> 0, of which waited for: 15 -> 0; matrix products, arithmetic and copies ran while one was open for 2% -> 0% of each run, Pallas kernels for 0% -> 0%
where the time goes in v1:
time: 53.9 us; the launch traced here: 53.8 us
  Pallas kernels  52.5 us (97%)
  between operations  0.66 us (1%)
  local copies, waits for them, and re-layouts  0.58 us (1%)
    pallas_call x1, Pallas kernels, local(): pl.pallas_call(functools.partial(kernel, n_row, n_col, n_row * width), ou...  52.5 us

profile of v1, /device:TPU:1, one launch (start us, length us, event | category | flops | bytes accessed | tf_op | source)
XLA Modules:
  0.0 53.8 jit_solution(2429622860508403445)
XLA Ops:
  0.7 52.5 %shard_map.46 = f32[4,128]{1,0:T(4,128)S(1)} custom-call(f32[4,128]{1,0:T(4,128)} %bitcast.6, f32[512,512]{1,0:T(8,128)} %bitcast.5, s32[1,1]{1,0:T(1,128)S(6)} %copy.7.reach_hbm, f32[1,32]{1,0:T(1,128)} %bitcast.7), custom_call_target="tpu_custom_call" | custom-call | tf_op jit(solution)/shard_map/pallas_call | solution.py:459
  53.2 0.6 %copy.6 = f32[1,1,1,512]{3,2,1,0:T(1,128)} copy(f32[1,1,1,512]{3,2,1,0:T(1,128)S(1)} %bitcast.4) | data formatting | bytes 4096

commit v2 on v1

--- a/solution.py
+++ b/solution.py
@@ -254,10 +254,10 @@
     weight_row_ref[...] = weight
 
     pl.semaphore_wait(barrier, 2 * (n_col - 1) + jnp.where(off_diagonal, chunks, 0))
+    for o in users:
+        push(z_ref, slab_ref.at[1, c], z_sent.at[0], z_col_sem.at[0], user(o))
     for o in peers:
         push(z_ref, slab_ref.at[0, c], z_sent.at[0], z_row_sem.at[0], peer(o))
-    for o in users:
-        push(z_ref, slab_ref.at[1, c], z_sent.at[0], z_col_sem.at[0], user(o))
 
     group, slot = lax.div(c, 4), lax.rem(c, 4)
     keeper = owner(r, group)

time: 53.9 us -> 53.7 us (level)
  no operation moved by 1% of the time
where the time goes in v2:
time: 53.7 us; the launch traced here: 53.6 us
  Pallas kernels  52.4 us (98%)
  between operations  0.66 us (1%)
  local copies, waits for them, and re-layouts  0.58 us (1%)
    pallas_call x1, Pallas kernels, local(): pl.pallas_call(functools.partial(kernel, n_row, n_col, n_row * width), ou...  52.4 us

profile of v2, /device:TPU:1, one launch (start us, length us, event | category | flops | bytes accessed | tf_op | source)
XLA Modules:
  0.0 53.6 jit_solution(4399336300754533609)
XLA Ops:
  0.7 52.4 %shard_map.46 = f32[4,128]{1,0:T(4,128)S(1)} custom-call(f32[4,128]{1,0:T(4,128)} %bitcast.6, f32[512,512]{1,0:T(8,128)} %bitcast.5, s32[1,1]{1,0:T(1,128)S(6)} %copy.7.reach_hbm, f32[1,32]{1,0:T(1,128)} %bitcast.7), custom_call_target="tpu_custom_call" | custom-call | tf_op jit(solution)/shard_map/pallas_call | solution.py:459
  53.0 0.6 %copy.6 = f32[1,1,1,512]{3,2,1,0:T(1,128)} copy(f32[1,1,1,512]{3,2,1,0:T(1,128)S(1)} %bitcast.4) | data formatting | bytes 4096

commit v3 on v2

--- a/solution.py
+++ b/solution.py
@@ -162,6 +162,7 @@
     load_sem,
     weight_sem,
     z_row_sem,
+    z_first_sem,
     z_col_sem,
     part_sem,
     gram_sem,
@@ -233,11 +234,6 @@
         for o in range(n_col):
             greet((j, o))
 
-    @pl.when(is_owner)
-    def _():
-        for o in users:
-            greet(user(o))
-
     for o in peers:
         greet(peer(o))
 
@@ -253,9 +249,10 @@
     slab_ref[0, c] = piece
     weight_row_ref[...] = weight
 
-    pl.semaphore_wait(barrier, 2 * (n_col - 1) + jnp.where(off_diagonal, chunks, 0))
+    pl.semaphore_wait(barrier, 2 * (n_col - 1))
+    owner_flag = jnp.where(is_owner, 1, 0)
     for o in users:
-        push(z_ref, slab_ref.at[1, c], z_sent.at[0], z_col_sem.at[0], user(o))
+        push(z_ref, slab_ref.at[1, c], z_sent.at[0], z_first_sem.at[owner_flag], user(o))
     for o in peers:
         push(z_ref, slab_ref.at[0, c], z_sent.at[0], z_row_sem.at[0], peer(o))
 
@@ -285,6 +282,8 @@
 
         @pl.when(off_diagonal)
         def _():
+            if sweep == 0:
+                wait_for(slab_ref.at[1, pl.ds(0, chunks)], z_first_sem.at[1])
             for turn in range(chunks):
                 i = lax.rem(d + turn, chunks)
                 push(
@@ -323,7 +322,7 @@
     def far_pieces():
         @pl.when(off_diagonal)
         def _():
-            wait_for(slab_ref.at[1], z_col_sem.at[0])
+            wait_for(slab_ref.at[1, pl.ds(0, n_col - chunks)], z_first_sem.at[0])
 
         return slab_to_vectors(slab_ref[side])
 
@@ -351,7 +350,7 @@
         for o in peers:
             push(chunk_ref, wide_ref.at[0, mine], z_sent.at[1], z_row_sem.at[1], peer(o))
         for o in users:
-            push(chunk_ref, wide_ref.at[1, mine], z_sent.at[1], z_col_sem.at[1], user(o))
+            push(chunk_ref, wide_ref.at[1, mine], z_sent.at[1], z_col_sem, user(o))
         gram_first_ref[...] = gram_spread(values)
         if chunks > 1:
             wait_for(wide_ref.at[0, pl.ds(0, chunks - 1)], z_row_sem.at[1])
@@ -363,7 +362,7 @@
     def far_chunks():
         @pl.when(off_diagonal)
         def _():
-            wait_for(wide_ref.at[1], z_col_sem.at[1])
+            wait_for(wide_ref.at[1], z_col_sem)
 
         return jnp.concatenate([wide_ref[side, i] for i in range(chunks)], axis=1)
 
@@ -488,6 +487,7 @@
             dma(()),
             dma((2,)),
             dma((2,)),
+            dma(()),
             dma((2,)),
             dma((2,)),
             dma(()),

time: 53.7 us -> 53.7 us (level)
  no operation moved by 1% of the time
where the time goes in v3:
time: 53.7 us; the launch traced here: 53.6 us
  Pallas kernels  52.3 us (97%)
  between operations  0.66 us (1%)
  local copies, waits for them, and re-layouts  0.58 us (1%)
    pallas_call x1, Pallas kernels, local(): pl.pallas_call(functools.partial(kernel, n_row, n_col, n_row * width), ou...  52.3 us

profile of v3, /device:TPU:1, one launch (start us, length us, event | category | flops | bytes accessed | tf_op | source)
XLA Modules:
  0.0 53.6 jit_solution(13152134030912948532)
XLA Ops:
  0.7 52.3 %shard_map.46 = f32[4,128]{1,0:T(4,128)S(1)} custom-call(f32[4,128]{1,0:T(4,128)} %bitcast.6, f32[512,512]{1,0:T(8,128)} %bitcast.5, s32[1,1]{1,0:T(1,128)S(6)} %copy.7.reach_hbm, f32[1,32]{1,0:T(1,128)} %bitcast.7), custom_call_target="tpu_custom_call" | custom-call | tf_op jit(solution)/shard_map/pallas_call | solution.py:458
  53.0 0.6 %copy.6 = f32[1,1,1,512]{3,2,1,0:T(1,128)} copy(f32[1,1,1,512]{3,2,1,0:T(1,128)S(1)} %bitcast.4) | data formatting | bytes 4096

commit v4 on v3

--- a/solution.py
+++ b/solution.py
@@ -271,12 +271,11 @@
     loads[3].wait()
     keep = jnp.where(d <= reach_ref[...], 1.0, 0.0) * jnp.where(r >= d, 1.0, 0.0)
     tile = tile_ref[...] * keep
-    high_ref[0], low_ref[0] = split(tile)
-    high_ref[1], low_ref[1] = split(jnp.transpose(tile))
+    high_ref[...], low_ref[...] = split(tile)
     lone = jnp.where(off_diagonal, 0.0, 1.0)
 
     def multiply(sweep, near, far_vectors):
-        mirror = dot_split(split(near), (high_ref[0], low_ref[0]), NN)
+        mirror = dot_split(split(near), (high_ref[...], low_ref[...]), NN)
         for i in range(chunks):
             far_ref[sweep, i] = mirror[:, 128 * i : 128 * i + 128]
 
@@ -294,7 +293,7 @@
                     (j, owner(j, i)),
                 )
 
-        forward = dot_split(split(far_vectors()), (high_ref[1], low_ref[1]), NN) + lone * mirror
+        forward = dot_split(split(far_vectors()), (high_ref[...], low_ref[...]), NT) + lone * mirror
         for i in range(chunks):
             own_ref[sweep, i] = forward[:, 128 * i : 128 * i + 128]
         for turn in range(chunks):
@@ -465,8 +464,8 @@
             pltpu.VMEM((width, width), F32),
             pltpu.VMEM((1, 1), jnp.int32),
             pltpu.VMEM((1, SUB), F32),
-            pltpu.VMEM((2, width, width), BF16),
-            pltpu.VMEM((2, width, width), BF16),
+            pltpu.VMEM((width, width), BF16),
+            pltpu.VMEM((width, width), BF16),
             pltpu.VMEM((1, 128), F32),
             pltpu.VMEM((4, 1, 128), F32),
             pltpu.VMEM((1, 128), F32),

time: 53.7 us -> 53.8 us (level)
  no operation moved by 1% of the time
where the time goes in v4:
time: 53.8 us; the launch traced here: 53.7 us
  Pallas kernels  52.4 us (97%)
  between operations  0.66 us (1%)
  local copies, waits for them, and re-layouts  0.58 us (1%)
    pallas_call x1, Pallas kernels, local(): pl.pallas_call(functools.partial(kernel, n_row, n_col, n_row * width), ou...  52.4 us

profile of v4, /device:TPU:1, one launch (start us, length us, event | category | flops | bytes accessed | tf_op | source)
XLA Modules:
  0.0 53.7 jit_solution(9940653374523499426)
XLA Ops:
  0.7 52.4 %shard_map.46 = f32[4,128]{1,0:T(4,128)S(1)} custom-call(f32[4,128]{1,0:T(4,128)} %bitcast.6, f32[512,512]{1,0:T(8,128)} %bitcast.5, s32[1,1]{1,0:T(1,128)S(6)} %copy.7.reach_hbm, f32[1,32]{1,0:T(1,128)} %bitcast.7), custom_call_target="tpu_custom_call" | custom-call | tf_op jit(solution)/shard_map/pallas_call | solution.py:457
  53.1 0.6 %copy.6 = f32[1,1,1,512]{3,2,1,0:T(1,128)} copy(f32[1,1,1,512]{3,2,1,0:T(1,128)S(1)} %bitcast.4) | data formatting | bytes 4096

commit v5 on v3

--- a/solution.py
+++ b/solution.py
@@ -67,9 +67,10 @@
     return fold_lanes(jnp.where(keep, wide, 0.0), (64, 32, 16))
 
 
-def rows_packed(spread):
+def rows_packed(spread, backward=False):
     shape = spread.shape
-    keep = iota(shape, 1) // 16 == iota(shape, 0) % 8
+    place = iota(shape, 0) % 8
+    keep = iota(shape, 1) // 16 == (7 - place if backward else place)
     held = jnp.where(keep, spread, 0.0)
     return jnp.concatenate(
         [jnp.sum(held[8 * a : 8 * a + 8], axis=0, keepdims=True) for a in range(shape[0] // 8)],
@@ -95,33 +96,39 @@
 
 def inverse_factor(gram):
     row = iota((8, 128), 0)
-    tops = [jnp.broadcast_to(gram[0:8, k : k + 1], (8, 128)) for k in range(K)]
-    bottoms = [jnp.broadcast_to(gram[8:16, k : k + 1], (8, 128)) for k in range(K)]
+    columns = [
+        [jnp.broadcast_to(gram[8 * half : 8 * half + 8, k : k + 1], (8, 128)) for k in range(K)]
+        for half in range(2)
+    ]
     unit = iota((8, 128), 1) % K
-    right = [jnp.where(unit == row, 1.0, 0.0), jnp.where(unit == row + 8, 1.0, 0.0)]
-    scale = [jnp.zeros((8, 128), F32), jnp.zeros((8, 128), F32)]
-    for step in range(K):
+    right = [jnp.where(unit == row + 8 * half, 1.0, 0.0) for half in range(2)]
+    done = []
+    for step in range(0, K, 2):
         half, place = step // 8, step % 8
-        here = (tops, bottoms)[half]
-        pivot = here[step][place : place + 1]
-        scale[half] = jnp.where(row == place, lax.rsqrt(pivot), scale[half])
-        if step == K - 1:
+        here = columns[half]
+        first = [here[k][place : place + 1] for k in range(K)]
+        second = [here[k][place + 1 : place + 2] for k in range(K)]
+        right_first = right[half][place : place + 1]
+        right_second = right[half][place + 1 : place + 2]
+        top, side, last = first[step], second[step], second[step + 1]
+        ratio = side / top
+        done.append(right_first * lax.rsqrt(top))
+        done.append((right_second - ratio * right_first) * lax.rsqrt(last - ratio * side))
+        if step == K - 2:
             break
-        inverse = 1.0 / pivot
-        lines = [here[k][place : place + 1] for k in range(K)]
-        right_line = right[half][place : place + 1]
-        if step < 7:
-            factor = jnp.where(row > place, tops[step] * inverse, 0.0)
-            for k in range(step + 1, K):
-                tops[k] = tops[k] - factor * lines[k]
-            right[0] = right[0] - factor * right_line
-        factor = bottoms[step] * inverse
-        if half == 1:
-            factor = jnp.where(row > place, factor, 0.0)
-        for k in range(step + 1, K):
-            bottoms[k] = bottoms[k] - factor * lines[k]
-        right[1] = right[1] - factor * right_line
-    return jnp.concatenate([right[0] * scale[0], right[1] * scale[1]], axis=0)
+        inverse = 1.0 / (top * last - side * side)
+        for part in range(half, 2):
+            one, two = columns[part][step], columns[part][step + 1]
+            factor_one = (last * one - side * two) * inverse
+            factor_two = (top * two - side * one) * inverse
+            if part == half:
+                below = row > place + 1
+                factor_one = jnp.where(below, factor_one, 0.0)
+                factor_two = jnp.where(below, factor_two, 0.0)
+            for k in range(step + 2, K):
+                columns[part][k] = columns[part][k] - (factor_one * first[k] + factor_two * second[k])
+            right[part] = right[part] - (factor_one * right_first + factor_two * right_second)
+    return jnp.concatenate(done, axis=0)
 
 
 def far_first(count, period):
@@ -162,6 +169,7 @@
     load_sem,
     weight_sem,
     z_row_sem,
+    z_near_sem,
     z_first_sem,
     z_col_sem,
     part_sem,
@@ -182,6 +190,9 @@
     j = lax.rem(r - d + n_row, n_row)
     off_diagonal = d != 0
     y_count = n_col // 2
+    per_half = min(2, chunks)
+    halves = chunks // per_half
+    span = 128 * per_half
 
     def owner(row, chunk):
         place = lax.rem(row, n_col)
@@ -189,6 +200,7 @@
         return x_low * y_count + lax.rem(place + y_count - 1 + 2 * lax.rem(chunk, 2), y_count)
 
     owners = [owner(r, i) for i in range(chunks)]
+    size = chunks // 2
     mine = sum(jnp.where(c == place, i, 0) for i, place in enumerate(owners))
     is_owner = functools.reduce(jnp.logical_or, [c == place for place in owners])
     not_owner = jnp.logical_not(is_owner)
@@ -254,7 +266,7 @@
     for o in users:
         push(z_ref, slab_ref.at[1, c], z_sent.at[0], z_first_sem.at[owner_flag], user(o))
     for o in peers:
-        push(z_ref, slab_ref.at[0, c], z_sent.at[0], z_row_sem.at[0], peer(o))
+        push(z_ref, slab_ref.at[0, c], z_sent.at[0], z_row_sem, peer(o))
 
     group, slot = lax.div(c, 4), lax.rem(c, 4)
     keeper = owner(r, group)
@@ -267,49 +279,56 @@
     def _():
         push(weight_row_ref, weight_parts_ref.at[slot], weight_sent, weight_sem, (r, keeper))
 
-    loads[2].wait()
     loads[3].wait()
-    keep = jnp.where(d <= reach_ref[...], 1.0, 0.0) * jnp.where(r >= d, 1.0, 0.0)
-    tile = tile_ref[...] * keep
+    tile = tile_ref[...]
     high_ref[0], low_ref[0] = split(tile)
     high_ref[1], low_ref[1] = split(jnp.transpose(tile))
+    loads[2].wait()
+    keep = jnp.where(d <= reach_ref[...], 1.0, 0.0) * jnp.where(r >= d, 1.0, 0.0)
     lone = jnp.where(off_diagonal, 0.0, 1.0)
 
-    def multiply(sweep, near, far_vectors):
-        mirror = dot_split(split(near), (high_ref[0], low_ref[0]), NN)
-        for i in range(chunks):
-            far_ref[sweep, i] = mirror[:, 128 * i : 128 * i + 128]
-
-        @pl.when(off_diagonal)
-        def _():
-            if sweep == 0:
-                wait_for(slab_ref.at[1, pl.ds(0, chunks)], z_first_sem.at[1])
-            for turn in range(chunks):
-                i = lax.rem(d + turn, chunks)
-                push(
-                    far_ref.at[sweep, i],
-                    parts_ref.at[sweep, n_col - 2 + d],
-                    far_sent.at[sweep],
-                    part_sem.at[sweep],
-                    (j, owner(j, i)),
-                )
-
-        forward = dot_split(split(far_vectors()), (high_ref[1], low_ref[1]), NN) + lone * mirror
-        for i in range(chunks):
-            own_ref[sweep, i] = forward[:, 128 * i : 128 * i + 128]
-        for turn in range(chunks):
-            i = lax.rem(c + turn, chunks)
-            place = owner(r, i)
-
-            @pl.when(c != place)
+    def multiply(sweep, mirror_half, far_vectors):
+        mirror = []
+        for part in range(halves):
+            lanes = slice(part * span, part * span + span)
+            mirror.append(mirror_half(lanes))
+            for i in range(per_half):
+                far_ref[sweep, part * per_half + i] = mirror[part][:, 128 * i : 128 * i + 128]
+
+            @pl.when(off_diagonal)
             def _():
-                push(
-                    own_ref.at[sweep, i],
-                    parts_ref.at[sweep, lax.rem(place - c + n_col, n_col) - 1],
-                    own_sent.at[sweep],
-                    part_sem.at[sweep],
-                    (r, place),
-                )
+                if sweep == 0 and part == 0:
+                    wait_for(slab_ref.at[1, pl.ds(0, chunks)], z_first_sem.at[1])
+                for turn in range(per_half):
+                    i = part * per_half + lax.rem(d + turn, per_half)
+                    push(
+                        far_ref.at[sweep, i],
+                        parts_ref.at[sweep, n_col - 2 + d],
+                        far_sent.at[sweep],
+                        part_sem.at[sweep],
+                        (j, owner(j, i)),
+                    )
+
+        pieces = split(far_vectors() * keep)
+        for part in range(halves):
+            lanes = slice(part * span, part * span + span)
+            forward = dot_split(pieces, (high_ref[1, :, lanes], low_ref[1, :, lanes]), NN)
+            forward = forward + lone * mirror[part]
+            for i in range(per_half):
+                own_ref[sweep, part * per_half + i] = forward[:, 128 * i : 128 * i + 128]
+            for turn in range(per_half):
+                i = part * per_half + lax.rem(c + turn, per_half)
+                place = owner(r, i)
+
+                @pl.when(c != place)
+                def _():
+                    push(
+                        own_ref.at[sweep, i],
+                        parts_ref.at[sweep, lax.rem(place - c + n_col, n_col) - 1],
+                        own_sent.at[sweep],
+                        part_sem.at[sweep],
+                        (r, place),
+                    )
 
     def total(sweep):
         wait_for(parts_ref.at[sweep], part_sem.at[sweep])
@@ -317,7 +336,7 @@
 
     side = jnp.where(off_diagonal, 1, 0)
 
-    wait_for(slab_ref.at[0, pl.ds(0, n_col - 1)], z_row_sem.at[0])
+    wait_for(slab_ref.at[0, pl.ds(0, n_col - 1)], z_row_sem)
 
     def far_pieces():
         @pl.when(off_diagonal)
@@ -326,7 +345,12 @@
 
         return slab_to_vectors(slab_ref[side])
 
-    multiply(0, slab_to_vectors(slab_ref[0]), far_pieces)
+    near = split(slab_to_vectors(slab_ref[0]) * keep)
+
+    def first_half(lanes):
+        return dot_split(near, (high_ref[0, :, lanes], low_ref[0, :, lanes]), NN)
+
+    multiply(0, first_half, far_pieces)
 
     @pl.when(is_owner)
     def _():
@@ -348,16 +372,34 @@
         chunk_ref[...] = scaled
         wide_ref[0, mine] = scaled
         for o in peers:
-            push(chunk_ref, wide_ref.at[0, mine], z_sent.at[1], z_row_sem.at[1], peer(o))
+            push(chunk_ref, wide_ref.at[0, mine], z_sent.at[1], z_near_sem.at[lax.div(mine, size)], peer(o))
         for o in users:
             push(chunk_ref, wide_ref.at[1, mine], z_sent.at[1], z_col_sem, user(o))
         gram_first_ref[...] = gram_spread(values)
-        if chunks > 1:
-            wait_for(wide_ref.at[0, pl.ds(0, chunks - 1)], z_row_sem.at[1])
-
-    @pl.when(not_owner)
-    def _():
-        wait_for(wide_ref.at[0], z_row_sem.at[1])
+
+    def near_part(part):
+        own_part = jnp.logical_and(is_owner, lax.div(mine, size) == part)
+
+        @pl.when(own_part)
+        def _():
+            if size > 1:
+                wait_for(wide_ref.at[0, pl.ds(0, size - 1)], z_near_sem.at[part])
+
+        @pl.when(jnp.logical_not(own_part))
+        def _():
+            wait_for(wide_ref.at[0, pl.ds(0, size)], z_near_sem.at[part])
+
+        vectors = split(jnp.concatenate([wide_ref[0, size * part + i] for i in range(size)], axis=1) * keep)
+        rows = pl.ds(pl.multiple_of(part * (128 * size), 128 * size), 128 * size)
+        return lambda lanes: dot_split(vectors, (high_ref[0, rows, lanes], low_ref[0, rows, lanes]), NN)
+
+    nearer = jnp.where(lax.div(c, y_count) == lax.div(home, y_count), 0, 1)
+    product = near_part(nearer)
+    early = [product(slice(part * span, part * span + span)) for part in range(halves)]
+    product = near_part(1 - nearer)
+
+    def second_half(lanes):
+        return early[lanes.start // span] + product(lanes)
 
     def far_chunks():
         @pl.when(off_diagonal)
@@ -366,12 +408,12 @@
 
         return jnp.concatenate([wide_ref[side, i] for i in range(chunks)], axis=1)
 
-    multiply(1, jnp.concatenate([wide_ref[0, i] for i in range(chunks)], axis=1), far_chunks)
+    multiply(1, second_half, far_chunks)
 
     @pl.when(is_owner)
     def _():
         values = total(1) * chunk_weight_ref[...]
-        gram = rows_packed(gram_spread(values) + EPS * gram_first_ref[...])
+        gram = rows_packed(gram_spread(values) + EPS * gram_first_ref[...], backward=True)
         gram_ref[0] = gram
         gram_row_ref[mine] = gram
         for o in peers:
@@ -408,8 +450,15 @@
 
     back = split(jnp.concatenate([back_ref[...]] * 4, axis=0))
     wait_for(gram_col_ref, gram_sem.at[1])
-    gram = rows_spread(gram_own + jnp.sum(gram_col_ref[...], axis=0))
-    diagonal = jnp.where(iota((16, 128), 1) % K == iota((16, 128), 0), EPS * EPS, 0.0)
+    total_gram = gram_own + jnp.sum(gram_col_ref[...], axis=0)
+    gram = jnp.concatenate(
+        [
+            pltpu.roll(jnp.broadcast_to(total_gram[i : i + 1], (8, 128)), K, 1, stride=K, stride_axis=0)
+            for i in range(2)
+        ],
+        axis=0,
+    )
+    diagonal = jnp.where(iota((16, 128), 1) == iota((16, 128), 0), EPS * EPS, 0.0)
     solver = inverse_factor(gram * (1.0 / states) + diagonal)
     wide = jnp.concatenate([solver] * 8, axis=0)
     wide = jnp.where(iota((128, 128), 0) // K == iota((128, 128), 1) // K, wide, 0.0)
@@ -485,6 +534,7 @@
             pltpu.VMEM((4, 128), F32),
             dma((4,)),
             dma(()),
+            dma(()),
             dma((2,)),
             dma((2,)),
             dma(()),

time: 53.7 us -> 53.6 us (level)
  no operation moved by 1% of the time
where the time goes in v5:
time: 53.6 us; the launch traced here: 53.5 us
  Pallas kernels  52.3 us (98%)
  between operations  0.66 us (1%)
  local copies, waits for them, and re-layouts  0.58 us (1%)
    pallas_call x1, Pallas kernels, local(): pl.pallas_call(functools.partial(kernel, n_row, n_col, n_row * width), ou...  52.3 us

profile of v5, /device:TPU:1, one launch (start us, length us, event | category | flops | bytes accessed | tf_op | source)
XLA Modules:
  0.0 53.5 jit_solution(15376424097485481485)
XLA Ops:
  0.7 52.3 %shard_map.46 = f32[4,128]{1,0:T(4,128)S(1)} custom-call(f32[4,128]{1,0:T(4,128)} %bitcast.6, f32[512,512]{1,0:T(8,128)} %bitcast.5, s32[1,1]{1,0:T(1,128)S(6)} %copy.7.reach_hbm, f32[1,32]{1,0:T(1,128)} %bitcast.7), custom_call_target="tpu_custom_call" | custom-call | tf_op jit(solution)/shard_map/pallas_call | solution.py:507
  52.9 0.6 %copy.6 = f32[1,1,1,512]{3,2,1,0:T(1,128)} copy(f32[1,1,1,512]{3,2,1,0:T(1,128)S(1)} %bitcast.4) | data formatting | bytes 4096

commit v6 on v5

--- a/solution.py
+++ b/solution.py
@@ -233,21 +233,20 @@
             ((x_hbm, x_ref), (weight_hbm, weight_ref), (reach_hbm, reach_ref), (tile_hbm, tile_ref))
         )
     ]
+    barrier = pltpu.get_barrier_semaphore()
+
+    def greet(device):
+        pl.semaphore_signal(barrier, inc=1, device_id=device, device_id_type=MESH)
+
+    @pl.when(off_diagonal)
+    def _():
+        for o in range(n_col):
+            greet((j, o))
+
+    for o in peers:
+        greet(peer(o))
     for load in loads:
         load.start()
-
-    barrier = pltpu.get_barrier_semaphore()
-
-    def greet(device):
-        pl.semaphore_signal(barrier, inc=1, device_id=device, device_id_type=MESH)
-
-    @pl.when(off_diagonal)
-    def _():
-        for o in range(n_col):
-            greet((j, o))
-
-    for o in peers:
-        greet(peer(o))
 
     loads[0].wait()
     loads[1].wait()
@@ -449,6 +448,40 @@
         wait_for(back_ref, back_sem)
 
     back = split(jnp.concatenate([back_ref[...]] * 4, axis=0))
+    wait_for(slab_ref.at[:, pl.ds(0, n_col - 1)], z_sent.at[0])
+
+    @pl.when(c != keeper)
+    def _():
+        wait_for(weight_row_ref, weight_sent)
+
+    for sweep in range(2):
+
+        @pl.when(off_diagonal)
+        def _():
+            wait_for(far_ref.at[sweep], far_sent.at[sweep])
+
+        @pl.when(is_owner)
+        def _():
+            if chunks > 1:
+                wait_for(own_ref.at[sweep, pl.ds(0, chunks - 1)], own_sent.at[sweep])
+
+        @pl.when(not_owner)
+        def _():
+            wait_for(own_ref.at[sweep], own_sent.at[sweep])
+
+    @pl.when(is_owner)
+    def _():
+        wait_for(parts_ref.at[0], z_sent.at[1])
+        wait_for(gram_col_ref.at[pl.ds(0, n_col - 1)], gram_sent.at[0])
+
+        @pl.when(mine == group)
+        def _():
+            wait_for(result_ref.at[pl.ds(0, 3)], back_sent)
+
+        @pl.when(mine != group)
+        def _():
+            wait_for(result_ref, back_sent)
+
     wait_for(gram_col_ref, gram_sem.at[1])
     total_gram = gram_own + jnp.sum(gram_col_ref[...], axis=0)
     gram = jnp.concatenate(
@@ -463,41 +496,7 @@
     wide = jnp.concatenate([solver] * 8, axis=0)
     wide = jnp.where(iota((128, 128), 0) // K == iota((128, 128), 1) // K, wide, 0.0)
     out_ref[...] = dot_split(back, split(wide), NT)[0:4]
-
-    wait_for(slab_ref.at[:, pl.ds(0, n_col - 1)], z_sent.at[0])
     wait_for(gram_col_ref, gram_sent.at[1])
-
-    @pl.when(c != keeper)
-    def _():
-        wait_for(weight_row_ref, weight_sent)
-
-    for sweep in range(2):
-
-        @pl.when(off_diagonal)
-        def _():
-            wait_for(far_ref.at[sweep], far_sent.at[sweep])
-
-        @pl.when(is_owner)
-        def _():
-            if chunks > 1:
-                wait_for(own_ref.at[sweep, pl.ds(0, chunks - 1)], own_sent.at[sweep])
-
-        @pl.when(not_owner)
-        def _():
-            wait_for(own_ref.at[sweep], own_sent.at[sweep])
-
-    @pl.when(is_owner)
-    def _():
-        wait_for(parts_ref.at[0], z_sent.at[1])
-        wait_for(gram_col_ref.at[pl.ds(0, n_col - 1)], gram_sent.at[0])
-
-        @pl.when(mine == group)
-        def _():
-            wait_for(result_ref.at[pl.ds(0, 3)], back_sent)
-
-        @pl.when(mine != group)
-        def _():
-            wait_for(result_ref, back_sent)
 
 
 def local(start_modes, tiles, reach, weights, n_row, n_col):

time: 53.6 us -> 53.6 us (level)
  no operation moved by 1% of the time
where the time goes in v6:
time: 53.6 us; the launch traced here: 53.5 us
  Pallas kernels  52.2 us (97%)
  between operations  0.66 us (1%)
  local copies, waits for them, and re-layouts  0.58 us (1%)
    pallas_call x1, Pallas kernels, local(): pl.pallas_call(functools.partial(kernel, n_row, n_col, n_row * width), ou...  52.2 us

profile of v6, /device:TPU:1, one launch (start us, length us, event | category | flops | bytes accessed | tf_op | source)
XLA Modules:
  0.0 53.5 jit_solution(11952220711769077555)
XLA Ops:
  0.7 52.2 %shard_map.46 = f32[4,128]{1,0:T(4,128)S(1)} custom-call(f32[4,128]{1,0:T(4,128)} %bitcast.6, f32[512,512]{1,0:T(8,128)} %bitcast.5, s32[1,1]{1,0:T(1,128)S(6)} %copy.7.reach_hbm, f32[1,32]{1,0:T(1,128)} %bitcast.7), custom_call_target="tpu_custom_call" | custom-call | tf_op jit(solution)/shard_map/pallas_call | solution.py:506
  52.9 0.6 %copy.6 = f32[1,1,1,512]{3,2,1,0:T(1,128)} copy(f32[1,1,1,512]{3,2,1,0:T(1,128)S(1)} %bitcast.4) | data formatting | bytes 4096
